TPU v7x, 512 devices: a whole 4x4x16 slice. The times are simulated.
512 devices in a mesh: ctx: 32 (over y, x, core), head: 16 (over z).
Axes of the slice: x: 4, y: 4, z: 16, core: 2. Of those that a mesh axis runs over, the one named last changes fastest.
Arguments:
- queries: bfloat16 [65536, 4096], P(('ctx', 'head')), may hold values from -128 to 128
- vis_feats: bfloat16 [16384, 8192], P('ctx', 'head'), may hold values from -16 to 16
- kv_weight: bfloat16 [8192, 1024], P('head'), may hold values from -0.044194174 to 0.044194174
- key_gain: float32 [128], replicated, may hold values from 0.1 to 1.9
- cross_mask: int32 [65536, 4], P('ctx'), may hold values 0 or 1
- image_tokens: int32 [4], replicated, may hold values from 1 to 512, 1280 in all
- image_owner: int32 [4], replicated, may hold values from 0 to 31, as said below
Outputs:
- attended: bfloat16 [65536, 4096], P(('ctx', 'head'))
Inputs may be any that keep to these rules, and one draw needn't show every extreme that they name: `image_tokens`: they sum to 1280; the largest is exactly 512. `image_owner`: four distinct context indices; the first and the last index of ctx always hold an image.
All inputs are finite; a program needn't handle non-finite values. No bound on the sum of `cross_mask` on one device may be relied on, other than what follows from the above.
Results may differ from a plain program's by a relative error of at most 0.0014.
The roundings to bfloat16 on the way count: a program that leaves them out, or rounds other values in their place, can miss the bound.
Values may be sent and summed in bfloat16 or wider, within the bound.
A program may use at most 64 MiB of HBM per device.

v0:
```python
import jax
import jax.numpy as jnp
from jax import lax
from jax.sharding import PartitionSpec as P

EPSILON = 1e-05
FLOOR_SCORE = -1e30


def swapped(value, axis, bit):
    mask = 2**bit
    pairs = [(source, source ^ mask) for source in range(lax.axis_size(axis))]
    return lax.ppermute(value, axis, pairs)


def from_root(shard, axis, root):
    return lax.dynamic_index_in_dim(lax.all_gather(shard, axis), root, 0, keepdims=False)


def normalize_keys(stacked, key_gain):
    raw_keys = stacked[..., 0, :, :]
    square_mean = jnp.mean(raw_keys * raw_keys, axis=-2, keepdims=True)
    normed = raw_keys * lax.rsqrt(square_mean + EPSILON) * key_gain[:, None]
    joined = jnp.stack([normed, stacked[..., 1, :, :]], axis=-3)
    return joined.astype(jnp.bfloat16)


def arrange_keys(received, image_tokens):
    cap_rows = received[0].shape[-1]
    count_img = len(received)
    img_ids = jnp.arange(count_img, dtype=jnp.int32)
    laid_out = jnp.concatenate(received, axis=-1)
    positions = jnp.arange(count_img * cap_rows, dtype=jnp.int32)[:, None]
    member = (positions // cap_rows == img_ids[None, :]) & (
        positions % cap_rows < image_tokens[None, :]
    )
    return (laid_out, member.astype(jnp.float32))


def attend_rows(query_rows, mask_rows, key_cols, value_cols, member):
    row_count = query_rows.shape[0]
    rows_per_block = min(512, row_count)
    count_of_blocks = row_count // rows_per_block
    blocked_queries = query_rows.reshape((count_of_blocks, rows_per_block) + query_rows.shape[1:])
    mask_blocks = mask_rows.reshape(count_of_blocks, rows_per_block, mask_rows.shape[1])
    factor = query_rows.shape[-1] ** (-0.5)
    member_rows = member.T

    def one_block(block_pair):
        query_block, mask_block = block_pair
        allowed = jnp.dot(mask_block.astype(jnp.float32), member_rows) > 0.5
        allowed = allowed[:, None, :]
        scores = (
            jnp.einsum("rnd,dk->rnk", query_block, key_cols, preferred_element_type=jnp.float32)
            * factor
        )
        largest = jnp.max(jnp.where(allowed, scores, FLOOR_SCORE), axis=-1, keepdims=True)
        weights = jnp.where(allowed, jnp.exp(scores - largest), 0.0)
        summed = jnp.sum(weights, axis=-1, keepdims=True)
        mixed_out = jnp.einsum(
            "rnk,dk->rnd",
            weights.astype(jnp.bfloat16),
            value_cols,
            preferred_element_type=jnp.float32,
        )
        return (mixed_out / jnp.maximum(summed, 1.0)).astype(jnp.bfloat16)

    return lax.map(one_block, (blocked_queries, mask_blocks)).reshape(query_rows.shape)


def shards(queries, vis_feats, kv_weight, key_gain, cross_mask, image_tokens, image_owner):
    head_count = lax.axis_size("head")
    head_index = lax.axis_index("head")
    count_img = image_owner.shape[0]
    width_kv = kv_weight.shape[1]
    head_dim = key_gain.shape[0]
    kv_heads = width_kv // (2 * head_dim)
    tok_rows = queries.shape[0]
    query_heads = queries.shape[1] // head_dim
    per_kv = head_count // kv_heads
    share_part = lax.psum_scatter(
        lax.dot_general(
            kv_weight, vis_feats, (((0,), (1,)), ((), ())), preferred_element_type=jnp.float32
        ),
        "head",
        scatter_dimension=0,
        tiled=True,
    )
    for bit_index in range(per_kv.bit_length() - 1):
        partner = swapped(share_part, "head", bit_index)
        low_half = (head_index >> bit_index) % 2 == 0
        share_part = jnp.where(
            low_half,
            jnp.concatenate([share_part, partner], 0),
            jnp.concatenate([partner, share_part], 0),
        )
    local_kv = normalize_keys(share_part.reshape(1, 2, head_dim, -1), key_gain)[0].reshape(
        2 * head_dim, -1
    )
    received = [
        from_root(local_kv, "ctx", image_owner[img_index]) for img_index in range(count_img)
    ]
    laid_out, member = arrange_keys(received, image_tokens)
    key_cols = laid_out[:head_dim]
    value_cols = laid_out[head_dim:]
    group_size = query_heads // head_count
    grouped = queries.reshape(tok_rows, head_count, group_size, head_dim)
    exchanged = lax.all_to_all(grouped, "head", split_axis=1, concat_axis=0, tiled=True)
    rows_all = exchanged.shape[0]
    flat_rows = exchanged.reshape(rows_all, exchanged.shape[2], head_dim)
    attended_heads = attend_rows(flat_rows, cross_mask, key_cols, value_cols, member).reshape(
        exchanged.shape
    )
    restored = lax.all_to_all(attended_heads, "head", split_axis=0, concat_axis=1, tiled=True)
    return restored.reshape(tok_rows, query_heads * head_dim)


def solution(mesh):
    return jax.shard_map(
        shards,
        mesh=mesh,
        in_specs=(
            P(("ctx", "head"), None),
            P("ctx", "head"),
            P("head", None),
            P(),
            P("ctx", None),
            P(),
            P(),
        ),
        out_specs=P(("ctx", "head"), None),
        check_vma=False,
    )
```

profile of v0, /device:TPU:32, one launch (start us, length us, event | category | flops | bytes accessed | tf_op | source)
XLA Modules:
  0.0 319.4 jit_solution(1120493429123971343)
XLA Ops:
  6.5 0.0 copy-start
  6.5 0.0 copy-start.4
  6.5 0.0 copy-start.1
  6.5 0.0 reduce-scatter.2.cloned.1.call-start
  6.5 1.2 copy-done
  7.8 3.1 fusion.77
  10.9 0.0 reduce-scatter.2.cloned.1.call-update
  10.9 0.0 copy-start.3
  10.9 0.0 all-gather.2.cloned.1.call-start
  11.0 77.3 %reduce-scatter.2.cloned.1.call-done = f32[64,512]{1,0:T(8,128)} async-done(((f32[1024,512]{1,0:T(8,128)}), f32[64,512]{1,0:T(8,128)}) %reduce-scatter.2.cloned.1.call-update) | async-done | bytes 131088 | tf_op jit(solution)/shard_map/reduce_scatter | solution.py:81
  88.3 2.6 collective-permute-start
  91.0 5.0 %collective-permute-done = f32[64,512]{1,0:T(8,128)S(1)} collective-permute-done((f32[64,512]{1,0:T(8,128)}, f32[64,512]{1,0:T(8,128)S(1)}, u32[]{:S(2)}, u32[]{:S(2)}) %collective-permute-start) | collective-permute-done | bytes 131104 | tf_op jit(solution)/shard_map/ppermute | solution.py:13
  95.9 1.0 maximum_select_fusion.1
  96.9 5.3 %collective-permute-start.1 = (f32[128,512]{1,0:T(8,128)S(1)}, f32[128,512]{1,0:T(8,128)S(1)}, u32[]{:S(2)}, u32[]{:S(2)}) collective-permute-start(f32[128,512]{1,0:T(8,128)S(1)} %maximum_select_fusion.1), channel_id=1, source_target_pairs={{0,2},{1,3},{2,0},{3,1},{4,6},{5,7},{6,4},{7,5},{8,10},{9,11},{10,... | collective-permute-start | bytes 786440 | tf_op jit(solution)/shard_map/ppermute | solution.py:13
  102.2 5.9 %collective-permute-done.1 = f32[128,512]{1,0:T(8,128)S(1)} collective-permute-done((f32[128,512]{1,0:T(8,128)S(1)}, f32[128,512]{1,0:T(8,128)S(1)}, u32[]{:S(2)}, u32[]{:S(2)}) %collective-permute-start.1) | collective-permute-done | bytes 262176 | tf_op jit(solution)/shard_map/ppermute | solution.py:13
  108.2 0.0 copy-done.4
  108.2 0.1 multiply_convert_fusion
  108.3 0.7 pad_maximum_fusion.1
  109.0 0.0 all-gather.2.cloned.1.call-update
  109.1 0.0 copy-done.1
  109.1 1.4 copy.16
  110.4 11.2 %all-to-all-start = ((bf16[128,16,2,128]{0,3,2,1:T(8,128)(2,1)}), bf16[128,16,2,128]{0,3,2,1:T(8,128)(2,1)S(1)}, u32[]{:S(2)}, u32[]{:S(2)}) async-start(bf16[128,16,2,128]{0,3,2,1:T(8,128)(2,1)} %bitcast.1), calls=%async_computation | async-start | bytes 2097152 | tf_op jit(solution)/shard_map/all_to_all | solution.py:108
  121.7 0.0 copy-done.3
  121.7 0.7 fusion.76
  129.9 26.7 %all-to-all-done = bf16[128,16,2,128]{0,3,2,1:T(8,128)(2,1)S(1)} async-done(((bf16[128,16,2,128]{0,3,2,1:T(8,128)(2,1)}), bf16[128,16,2,128]{0,3,2,1:T(8,128)(2,1)S(1)}, u32[]{:S(2)}, u32[]{:S(2)}) %all-to-all-start) | async-done | bytes 1048608 | tf_op jit(solution)/shard_map/all_to_all | solution.py:108
  156.6 0.0 copy-start.5
  156.6 0.7 copy.17
  157.2 0.0 copy-start.2
  157.2 20.1 %all-gather.2.cloned.1.call-done = bf16[32,256,512]{2,1,0:T(8,128)(2,1)} async-done(((bf16[1,256,512]{2,1,0:T(8,128)(2,1)}), bf16[32,256,512]{2,1,0:T(8,128)(2,1)}) %all-gather.2.cloned.1.call-update) | async-done | bytes 8388624 | tf_op jit(solution)/shard_map/all_gather | solution.py:17
  177.3 1.3 dynamic-slice_bitcast_fusion.3
  178.6 0.1 pad_maximum_fusion
  178.7 1.0 fusion.75
  179.7 0.0 copy-done.5
  179.7 0.0 copy-done.2
  179.7 57.3 %while.11 = (s32[]{:T(128)}, bf16[4,512,2,128]{3,1,0,2:T(8,128)(2,1)S(1)}, s32[4,512,4]{1,2,0:T(4,128)}, bf16[4,512,2,128]{3,1,0,2:T(8,128)(2,1)S(1)}, bf16[128,...) while((s32[]{:T(128)}, ...), condition=%wide.region_5.6_spmd.clone, body=%wide.region_2.5_spmd.clone.sunk | while | flops 1635030016 | bytes 13936249 | solution.py:68
  179.7 2.5 convolution_compare_fusion.2
  182.2 8.2 %fusion.99 = (f32[512,2]{0,1:T(2,128)S(1)}, bf16[512,2,2048]{2,0,1:T(8,128)(2,1)}) fusion(pred[512,2048]{1,0:T(8,128)(4,1)} %convolution_compare_fusion.2, bf16[128,2048]{1,0:T(8,128)(2,1)} %get-tuple-element.210, bf16[4,512,2,128]{3,1,0,2:T(8,128)(2,1)S(1)} %get-tuple-element.209, s32[]{:T(128)} %get-tuple-element.196), kind=kOutput, calls=%fused_computation.64.clone.1 | convolution fusion | flops 1088423936 | bytes 7869440 | tf_op jit(solution)/shard_map/while/body/eval_jaxpr/sub | solution.py:58
  190.4 3.7 %fusion.100 = bf16[4,512,2,128]{3,1,0,2:T(8,128)(2,1)S(1)} fusion(bf16[4,512,2,128]{3,1,0,2:T(8,128)(2,1)S(1)} %get-tuple-element.197, s32[]{:T(128)} %get-tuple-element.196, bf16[512,2,2048]{2,0,1:T(8,128)(2,1)} %get-tuple-element.184, bf16[128,2048]{1,0:T(8,128)(2,1)} %get-tuple-element.211, f32[512,2]{0,1:T(2,128)S(1)} %broadcast_maximum_fusion.2), kind=kOutput, calls=%fused_computation.15.clone.1 | convolution fusion | flops 537133056 | bytes 4984836 | tf_op jit(solution)/shard_map/while/body/eval_jaxpr/rnk,dk->rnd/dot_general | solution.py:60
  194.1 2.5 convolution_compare_fusion.2
  196.6 8.2 %fusion.99 = (f32[512,2]{0,1:T(2,128)S(1)}, bf16[512,2,2048]{2,0,1:T(8,128)(2,1)}) fusion(pred[512,2048]{1,0:T(8,128)(4,1)} %convolution_compare_fusion.2, bf16[128,2048]{1,0:T(8,128)(2,1)} %get-tuple-element.210, bf16[4,512,2,128]{3,1,0,2:T(8,128)(2,1)S(1)} %get-tuple-element.209, s32[]{:T(128)} %get-tuple-element.196), kind=kOutput, calls=%fused_computation.64.clone.1 | convolution fusion | flops 1088423936 | bytes 7869440 | tf_op jit(solution)/shard_map/while/body/eval_jaxpr/sub | solution.py:58
  204.7 3.7 %fusion.100 = bf16[4,512,2,128]{3,1,0,2:T(8,128)(2,1)S(1)} fusion(bf16[4,512,2,128]{3,1,0,2:T(8,128)(2,1)S(1)} %get-tuple-element.197, s32[]{:T(128)} %get-tuple-element.196, bf16[512,2,2048]{2,0,1:T(8,128)(2,1)} %get-tuple-element.184, bf16[128,2048]{1,0:T(8,128)(2,1)} %get-tuple-element.211, f32[512,2]{0,1:T(2,128)S(1)} %broadcast_maximum_fusion.2), kind=kOutput, calls=%fused_computation.15.clone.1 | convolution fusion | flops 537133056 | bytes 4984836 | tf_op jit(solution)/shard_map/while/body/eval_jaxpr/rnk,dk->rnd/dot_general | solution.py:60
  208.4 2.5 convolution_compare_fusion.2
  210.9 8.2 %fusion.99 = (f32[512,2]{0,1:T(2,128)S(1)}, bf16[512,2,2048]{2,0,1:T(8,128)(2,1)}) fusion(pred[512,2048]{1,0:T(8,128)(4,1)} %convolution_compare_fusion.2, bf16[128,2048]{1,0:T(8,128)(2,1)} %get-tuple-element.210, bf16[4,512,2,128]{3,1,0,2:T(8,128)(2,1)S(1)} %get-tuple-element.209, s32[]{:T(128)} %get-tuple-element.196), kind=kOutput, calls=%fused_computation.64.clone.1 | convolution fusion | flops 1088423936 | bytes 7869440 | tf_op jit(solution)/shard_map/while/body/eval_jaxpr/sub | solution.py:58
  219.1 3.7 %fusion.100 = bf16[4,512,2,128]{3,1,0,2:T(8,128)(2,1)S(1)} fusion(bf16[4,512,2,128]{3,1,0,2:T(8,128)(2,1)S(1)} %get-tuple-element.197, s32[]{:T(128)} %get-tuple-element.196, bf16[512,2,2048]{2,0,1:T(8,128)(2,1)} %get-tuple-element.184, bf16[128,2048]{1,0:T(8,128)(2,1)} %get-tuple-element.211, f32[512,2]{0,1:T(2,128)S(1)} %broadcast_maximum_fusion.2), kind=kOutput, calls=%fused_computation.15.clone.1 | convolution fusion | flops 537133056 | bytes 4984836 | tf_op jit(solution)/shard_map/while/body/eval_jaxpr/rnk,dk->rnd/dot_general | solution.py:60
  222.8 2.5 convolution_compare_fusion.2
  225.3 8.2 %fusion.99 = (f32[512,2]{0,1:T(2,128)S(1)}, bf16[512,2,2048]{2,0,1:T(8,128)(2,1)}) fusion(pred[512,2048]{1,0:T(8,128)(4,1)} %convolution_compare_fusion.2, bf16[128,2048]{1,0:T(8,128)(2,1)} %get-tuple-element.210, bf16[4,512,2,128]{3,1,0,2:T(8,128)(2,1)S(1)} %get-tuple-element.209, s32[]{:T(128)} %get-tuple-element.196), kind=kOutput, calls=%fused_computation.64.clone.1 | convolution fusion | flops 1088423936 | bytes 7869440 | tf_op jit(solution)/shard_map/while/body/eval_jaxpr/sub | solution.py:58
  233.4 3.7 %fusion.100 = bf16[4,512,2,128]{3,1,0,2:T(8,128)(2,1)S(1)} fusion(bf16[4,512,2,128]{3,1,0,2:T(8,128)(2,1)S(1)} %get-tuple-element.197, s32[]{:T(128)} %get-tuple-element.196, bf16[512,2,2048]{2,0,1:T(8,128)(2,1)} %get-tuple-element.184, bf16[128,2048]{1,0:T(8,128)(2,1)} %get-tuple-element.211, f32[512,2]{0,1:T(2,128)S(1)} %broadcast_maximum_fusion.2), kind=kOutput, calls=%fused_computation.15.clone.1 | convolution fusion | flops 537133056 | bytes 4984836 | tf_op jit(solution)/shard_map/while/body/eval_jaxpr/rnk,dk->rnd/dot_general | solution.py:60
  237.1 8.7 %copy.20 = bf16[2048,1,2,128]{3,2,1,0:T(2,128)(2,1)S(1)} copy(bf16[2048,1,2,128]{3,0,2,1:T(8,128)(2,1)S(1)} %bitcast.89) | data formatting | bytes 2097152 | tf_op jit(solution)/shard_map/reshape;reshape | solution.py:111
  245.8 64.6 %all_to_all.30 = bf16[2048,1,2,128]{3,2,1,0:T(2,128)(2,1)S(1)} all-to-all(bf16[2048,1,2,128]{3,2,1,0:T(2,128)(2,1)S(1)} %copy.20), channel_id=1, replica_groups=mesh['ctx'=32,'head'=16] {'head'}, dimensions={0} | all-to-all | bytes 2097152 | tf_op jit(solution)/shard_map/all_to_all | solution.py:114
  310.4 0.1 copy.21
  310.6 0.7 copy.22
  311.2 1.3 copy.23
  (10 shorter events, 0.1 us)
Async XLA Ops:
  6.5 1.2 copy-start
  6.5 101.7 %copy-start.4 = (f32[128]{0:T(128)S(1)}, f32[128]{0:T(128)}, u32[]{:S(2)}) copy-start(f32[128]{0:T(128)} %param.12) | copy-start | bytes 1540
  6.5 102.5 %copy-start.1 = (bf16[128,4096]{1,0:T(8,128)(2,1)S(1)}, bf16[128,4096]{1,0:T(8,128)(2,1)}, u32[]{:S(2)}) copy-start(bf16[128,4096]{1,0:T(8,128)(2,1)} %param.9) | copy-start | bytes 3145732
  6.5 81.7 %reduce-scatter.2.cloned.1.call-start = ((), (), s32[]{:S(2)}) async-start(), calls=%async_computation.3 | async-start | bytes 2228224 | tf_op jit(solution)/shard_map/reduce_scatter | solution.py:81
  10.9 110.7 %copy-start.3 = (s32[4]{0:T(128)S(1)}, s32[4]{0:T(128)}, u32[]{:S(2)}) copy-start(s32[4]{0:T(128)} %param.15) | copy-start | bytes 52
  10.9 166.4 %all-gather.2.cloned.1.call-start = ((), (), s32[]{:S(2)}) async-start(), calls=%async_computation.4 | async-start | bytes 8650752 | tf_op jit(solution)/shard_map/all_gather | solution.py:17
  88.3 7.6 %collective-permute-start = (f32[64,512]{1,0:T(8,128)}, f32[64,512]{1,0:T(8,128)S(1)}, u32[]{:S(2)}, u32[]{:S(2)}) collective-permute-start(f32[64,512]{1,0:T(8,128)} %reduce-scatter.2.cloned.1.call-done), channel_id=1, source_target_pairs={{0,1},{1,0},{2,3},{3,2},{4,5},{5,4},{6,7},{7,6},{8,9},{9,8},{10,11... | collective-permute-start | bytes 393224 | tf_op jit(solution)/shard_map/ppermute | solution.py:13
  96.9 11.1 %collective-permute-start.1 = (f32[128,512]{1,0:T(8,128)S(1)}, f32[128,512]{1,0:T(8,128)S(1)}, u32[]{:S(2)}, u32[]{:S(2)}) collective-permute-start(f32[128,512]{1,0:T(8,128)S(1)} %maximum_select_fusion.1), channel_id=1, source_target_pairs={{0,2},{1,3},{2,0},{3,1},{4,6},{5,7},{6,4},{7,5},{8,10},{9,11},{10,... | collective-permute-start | bytes 786440 | tf_op jit(solution)/shard_map/ppermute | solution.py:13
  110.4 46.1 %all-to-all-start = ((bf16[128,16,2,128]{0,3,2,1:T(8,128)(2,1)}), bf16[128,16,2,128]{0,3,2,1:T(8,128)(2,1)S(1)}, u32[]{:S(2)}, u32[]{:S(2)}) async-start(bf16[128,16,2,128]{0,3,2,1:T(8,128)(2,1)} %bitcast.1), calls=%async_computation | async-start | bytes 2097152 | tf_op jit(solution)/shard_map/all_to_all | solution.py:108
  156.6 23.2 %copy-start.5 = (s32[4]{0:T(128)S(1)}, s32[4]{0:T(128)}, u32[]{:S(2)}) copy-start(s32[4]{0:T(128)} %param.14) | copy-start | bytes 52
  157.2 22.5 %copy-start.2 = (bf16[4,512,2,128]{3,1,0,2:T(8,128)(2,1)S(1)}, bf16[4,512,2,128]{3,1,0,2:T(8,128)(2,1)}, u32[]{:S(2)}) copy-start(bf16[4,512,2,128]{3,1,0,2:T(8,128)(2,1)} %custom-call) | copy-start | bytes 3145732
Sparse Core Ops, SparseCore 0:
  11.0 77.1 reduce-scatter.1
  109.2 68.0 all-gather.1
where the time goes:
time: 320 us; the launch traced here: 319 us
  waiting for transfers between devices  135 us (42%)
  blocking collectives  64.6 us (20%)
  matrix products  60.4 us (19%)
  between operations  21.1 us (7%)
  starting transfers between devices  19.2 us (6%)
  local copies, waits for them, and re-layouts  17 us (5%)
    reduce_scatter x1, waiting for transfers between devices, shards(): lax.psum_scatter(lax.dot_general(kv_weight, vis_feats, (((0,), (1,)), (()...  77.3 us
    all_to_all x1, blocking collectives, shards(): lax.all_to_all(attended_heads, 'head', split_axis=0, concat_axis=1, tiled...  64.6 us
    sub x4, matrix products, one_block(): weights = jnp.where(allowed, jnp.exp(scores - largest), 0.0)  32.7 us
    all_to_all x1, waiting for transfers between devices, shards(): lax.all_to_all(grouped, 'head', split_axis=1, concat_axis=0, tiled=True)  26.7 us
    all_gather x1, waiting for transfers between devices, from_root(): lax.all_gather(shard, axis)  20.1 us
    dot_general x4, matrix products, one_block(): jnp.einsum('rnk,dk->rnd', weights.astype(jnp.bfloat16), value_cols, prefe...  14.6 us
    all_to_all x1, starting transfers between devices, shards(): lax.all_to_all(grouped, 'head', split_axis=1, concat_axis=0, tiled=True)  11.2 us
    ppermute x2, waiting for transfers between devices, swapped(): return lax.ppermute(value, axis, pairs)  10.8 us
  transfers between devices with their start and end apart: 5, of which 5 were waited for; matrix products, arithmetic and copies ran while one was open for 1% of the time, Pallas kernels for 0%

commit v1 on v0

v1 whole, which is shorter than its diff:
```python
import functools
import math

import jax
import jax.numpy as jnp
from jax import lax
from jax.experimental import pallas as pl
from jax.experimental.pallas import tpu as pltpu
from jax.sharding import PartitionSpec as P

EPSILON = 1e-05
FLOOR_SCORE = -1e30
MASKED = -(2.0**120)
HEAD = 128
PACKED = 1280


def packed_index(image_tokens):
    images = jnp.arange(image_tokens.shape[0], dtype=jnp.int32)
    earlier = images[None, :] < images[:, None]
    starts = jnp.sum(jnp.where(earlier, image_tokens[None, :], 0), axis=1)
    ends = starts + image_tokens
    place = jnp.arange(PACKED, dtype=jnp.int32)
    image = jnp.sum((place[:, None] >= ends[None, :]).astype(jnp.int32), axis=1)
    onehot = image[:, None] == images[None, :]
    token = place - jnp.sum(jnp.where(onehot, starts[None, :], 0), axis=1)
    return onehot, token


def attend_kernel(group, q_ref, kv_ref, mask_ref, hot_ref, o_ref, keys):
    rows = q_ref.shape[0]
    heads = kv_ref.shape[1] // (2 * HEAD)
    per_step = 4
    factor = HEAD**-0.5 * math.log2(math.e)
    bias = mask_ref[...]
    keys[:, HEAD:] = hot_ref[...]
    for head in range(heads):
        keys[:, :HEAD] = kv_ref[:, 2 * head * HEAD : (2 * head + 1) * HEAD]
        values = kv_ref[:, (2 * head + 1) * HEAD : (2 * head + 2) * HEAD]

        def step(i, carry):
            base = pl.multiple_of((head * group + i * per_step) * HEAD, HEAD)
            stacked = jnp.concatenate(
                [
                    jnp.concatenate([q_ref[:, pl.ds(base + j * HEAD, HEAD)], bias], axis=1)
                    for j in range(per_step)
                ],
                axis=0,
            )
            scores = lax.dot_general(
                stacked, keys[...], (((1,), (1,)), ((), ())), preferred_element_type=jnp.float32
            )
            largest = jnp.maximum(jnp.max(scores, axis=1, keepdims=True), FLOOR_SCORE)
            weights = jnp.exp2(scores * factor - largest * factor)
            summed = jnp.sum(weights, axis=1, keepdims=True)
            mixed = jnp.dot(weights.astype(jnp.bfloat16), values, preferred_element_type=jnp.float32)
            out = (mixed / jnp.maximum(summed, 1.0)).astype(jnp.bfloat16)
            for j in range(per_step):
                o_ref[:, pl.ds(base + j * HEAD, HEAD)] = out[j * rows : (j + 1) * rows]
            return carry

        lax.fori_loop(0, group // per_step, step, 0)


def attend(queries, kv, bias, hot, group):
    return pl.pallas_call(
        functools.partial(attend_kernel, group),
        out_shape=jax.ShapeDtypeStruct(queries.shape, jnp.bfloat16),
        in_specs=[pl.BlockSpec(memory_space=pltpu.VMEM)] * 4,
        out_specs=pl.BlockSpec(memory_space=pltpu.VMEM),
        scratch_shapes=[pltpu.VMEM((PACKED, 2 * HEAD), jnp.bfloat16)],
        compiler_params=pltpu.CompilerParams(vmem_limit_bytes=56 * 1024 * 1024),
        name="attend",
    )(queries, kv, bias, hot)


def shards(queries, vis_feats, kv_weight, key_gain, cross_mask, image_tokens, image_owner):
    ctx, z = lax.axis_index("ctx"), lax.axis_index("head")
    rows = queries.shape[0]
    onehot, token = packed_index(image_tokens)
    owned = jnp.sum(jnp.where(onehot, image_owner[None, :], 0), axis=1) == ctx
    slots = jnp.arange(vis_feats.shape[0], dtype=jnp.int32)
    select = (token[:, None] == slots[None, :]) & owned[:, None]
    contribution = jnp.dot(
        select.astype(jnp.bfloat16), vis_feats, preferred_element_type=jnp.float32
    ).astype(jnp.bfloat16)
    mine = lax.psum_scatter(contribution, "ctx", scatter_dimension=0, tiled=True)
    partial = jnp.dot(mine, kv_weight, preferred_element_type=jnp.float32)
    projected = lax.psum(partial, "head").reshape(mine.shape[0], -1, 2, HEAD)
    raw = projected[:, :, 0]
    scale = lax.rsqrt(jnp.mean(raw * raw, axis=-1, keepdims=True) + EPSILON)
    normed = raw * scale * key_gain
    kv = jnp.stack([normed, projected[:, :, 1]], axis=2).astype(jnp.bfloat16)
    kv = lax.all_gather(kv.reshape(mine.shape[0], -1), "ctx", axis=0, tiled=True)
    mask_rows = lax.dynamic_slice_in_dim(cross_mask, z * rows, rows, 0)
    bias = jnp.where(mask_rows == 1, 0.0, MASKED).astype(jnp.bfloat16)
    pad = ((0, 0), (0, HEAD - bias.shape[1]))
    bias = jnp.pad(bias, pad)
    hot = jnp.pad(onehot.astype(jnp.bfloat16), pad)
    group = queries.shape[1] // HEAD // (kv_weight.shape[1] // (2 * HEAD))
    return attend(queries, kv, bias, hot, group)


def solution(mesh):
    return jax.shard_map(
        shards,
        mesh=mesh,
        in_specs=(
            P(("ctx", "head"), None),
            P("ctx", "head"),
            P("head", None),
            P(),
            P("ctx", None),
            P(),
            P(),
        ),
        out_specs=P(("ctx", "head"), None),
        check_vma=False,
    )
```

time: 320 us -> 342 us (1.069)
  the two profiles are of different devices: /device:TPU:32 before, /device:TPU:1 now
where the time goes in v1:
time: 342 us
  waiting for transfers between devices  295 us (86%)
  Pallas kernels  18.5 us (5%)
  between operations  13.2 us (4%)
  other arithmetic  6.53 us (2%)
  matrix products  4.44 us (1%)
  local copies, waits for them, and re-layouts  3.92 us (1%)
    psum x1, waiting for transfers between devices, shards(): projected = lax.psum(partial, 'head').reshape(mine.shape[0], -1, 2, HEAD)  126 us
    reduce_scatter x1, waiting for transfers between devices, shards(): lax.psum_scatter(contribution, 'ctx', scatter_dimension=0, tiled=True)  105 us
    all_gather x1, waiting for transfers between devices, shards(): lax.all_gather(kv.reshape(mine.shape[0], -1), 'ctx', axis=0, tiled=True)  63.9 us
    pallas_call x1, Pallas kernels, attend(): pl.pallas_call(functools.partial(attend_kernel, group), out_shape=jax.Sha...  18.5 us
  transfers between devices with their start and end apart: 3, of which 3 were waited for; matrix products, arithmetic and copies ran while one was open for 1% of the time, Pallas kernels for 0%

profile of v1, /device:TPU:1, one launch (start us, length us, event | category | flops | bytes accessed | tf_op | source)
XLA Modules:
  0.0 341.9 jit_solution(9096976735571694140)
XLA Ops:
  6.5 0.0 copy-start
  6.5 0.0 reduce-scatter.2.cloned.1.call-start
  6.5 0.9 select_reduce_fusion.2
  7.4 0.7 add.23
  8.1 0.1 convert_reduce_fusion
  8.1 1.3 select_reduce_fusion
  9.4 0.0 copy-start.1
  9.4 3.4 convolution_convert_fusion
  12.8 0.0 reduce-scatter.2.cloned.1.call-update
  12.8 0.0 all-reduce.4.cloned.1.call-start
  12.9 104.9 %reduce-scatter.2.cloned.1.call-done = bf16[40,512]{1,0:T(8,128)(2,1)} async-done(((bf16[1280,512]{1,0:T(8,128)(2,1)}), bf16[40,512]{1,0:T(8,128)(2,1)}) %reduce-scatter.2.cloned.1.call-update) | async-done | bytes 40976 | tf_op jit(solution)/shard_map/reduce_scatter | solution.py:87
  117.8 0.0 copy-done
  117.8 1.1 fusion.4
  118.8 0.8 reshape.30
  119.6 0.0 all-reduce.4.cloned.1.call-update
  119.7 0.0 all-gather.2.cloned.1.call-start
  119.7 126.4 %all-reduce.4.cloned.1.call-done = f32[40,4,2,128]{3,2,1,0:T(2,128)} async-done(((f32[40,4,2,128]{3,2,1,0:T(2,128)}), f32[40,4,2,128]{3,2,1,0:T(2,128)}) %all-reduce.4.cloned.1.call-update) | async-done | bytes 163856 | tf_op jit(solution)/shard_map/psum | solution.py:89
  246.1 1.2 multiply_reduce_fusion
  247.4 1.0 slice.14
  248.4 0.0 copy-done.1
  248.4 1.2 multiply_convert_fusion
  249.6 0.2 pad_maximum_fusion
  249.8 0.7 convert_element_type.22
  250.4 0.0 all-gather.2.cloned.1.call-update
  250.5 0.7 constant_dynamic-slice_fusion
  251.2 0.1 copy.10
  251.3 0.6 pad.10.mask_ref
  251.9 0.2 iota_compare_fusion.1
  252.1 0.8 pad_convert_fusion.hot_ref
  252.9 63.9 %all-gather.2.cloned.1.call-done.kv_ref = bf16[1280,1024]{1,0:T(8,128)(2,1)} async-done(((bf16[40,1024]{1,0:T(8,128)(2,1)}), bf16[1280,1024]{1,0:T(8,128)(2,1)}) %all-gather.2.cloned.1.call-update) | async-done | bytes 2621456 | tf_op jit(solution)/shard_map/all_gather | solution.py:94
  316.9 18.5 %attend.1 = bf16[128,4096]{1,0:T(8,128)(2,1)} custom-call(bf16[128,4096]{1,0:T(8,128)(2,1)} %q_ref.1, bf16[1280,1024]{1,0:T(8,128)(2,1)} %all-gather.2.cloned.1.call-done.kv_ref, bf16[128,128]{1,0:T(8,128)(2,1)} %pad.10.mask_ref, bf16[1280,128]{1,0:T(8,128)(2,1)} %pad_convert_fusion.hot_ref), custom_call_target="tpu_custom_call" | custom-call | tf_op jit(solution)/shard_map/attend/pallas_call | solution.py:66
  (4 shorter events, 0.0 us)
Async XLA Ops:
  6.5 111.2 %copy-start = (bf16[512,1024]{1,0:T(8,128)(2,1)S(1)}, bf16[512,1024]{1,0:T(8,128)(2,1)}, u32[]{:S(2)}) copy-start(bf16[512,1024]{1,0:T(8,128)(2,1)} %param.9) | copy-start | bytes 3145732
  6.5 111.2 %reduce-scatter.2.cloned.1.call-start = ((), (), s32[]{:S(2)}) async-start(), calls=%async_computation.1 | async-start | bytes 1351680 | tf_op jit(solution)/shard_map/reduce_scatter | solution.py:87
  9.4 239.0 %copy-start.1 = (f32[128]{0:T(128)S(1)}, f32[128]{0:T(128)}, u32[]{:S(2)}) copy-start(f32[128]{0:T(128)} %param.10) | copy-start | bytes 1540
  12.8 233.3 %all-reduce.4.cloned.1.call-start = ((), (), s32[]{:S(2)}) async-start(), calls=%async_computation.2 | async-start | bytes 327680 | tf_op jit(solution)/shard_map/psum | solution.py:89
  119.7 197.2 %all-gather.2.cloned.1.call-start = ((), (), s32[]{:S(2)}) async-start(), calls=%async_computation.3 | async-start | bytes 2703360 | tf_op jit(solution)/shard_map/all_gather | solution.py:94
Sparse Core Ops, SparseCore 0:
  13.0 104.7 reduce-scatter.1
  120.2 125.8 all-reduce.3
  250.6 66.2 all-gather.1

commit v2 on v1

v2 whole, which is shorter than its diff:
```python
import math

import jax
import jax.numpy as jnp
from jax import lax
from jax.experimental import pallas as pl
from jax.experimental.pallas import tpu as pltpu
from jax.sharding import PartitionSpec as P

EPSILON = 1e-05
FLOOR_SCORE = -1e30
MASKED = -(2.0**120)
HEAD = 128
SIDE = 4
DEPTH = 16
SHARE = 80
PACKED = SHARE * SIDE * SIDE
GROUP = 8
STEP_HEADS = 4
MESH = pl.DeviceIdType.MESH
BF16, F32 = jnp.bfloat16, jnp.float32


def kernel(
    tokens_ref, owner_ref, feats_ref, weight_ref, gain_ref, mask_ref, q_ref, o_ref,
    own, sib, first_in, first_sum, second_in, chip_feats, part, part_in, done, kv, hot, keys,
    sib_s, sib_r, first_s, first_r, second_s, second_r, pair_s, pair_r,
    part_s, part_r, column_s, column_r, row_s, row_r, plane_s, plane_r, twin_s, twin_r,
):
    ctx, z = lax.axis_index("ctx"), lax.axis_index("head")
    core = lax.rem(ctx, 2)
    x = lax.rem(lax.div(ctx, 2), SIDE)
    y = lax.div(ctx, 2 * SIDE)
    a = x * (1 - core) + y * core
    b = y * (1 - core) + x * core

    def at(x_to, y_to, core_to, z_to):
        return {"ctx": (y_to * SIDE + x_to) * 2 + core_to, "head": z_to}

    def along_a(d):
        to = lax.rem(a + d, SIDE)
        return at(to * (1 - core) + x * core, y * (1 - core) + to * core, core, z)

    def along_b(d):
        to = lax.rem(b + d, SIDE)
        return at(x * (1 - core) + to * core, to * (1 - core) + y * core, core, z)

    def along_z(d):
        return at(x, y, core, lax.rem(z + d, DEPTH))

    twin = at(x, y, 1 - core, z)

    def chip_of(which, a_to, b_to):
        return (a_to * SIDE + b_to) * (1 - which) + (b_to * SIDE + a_to) * which

    def copy(src, dst, send, recv, device):
        return pltpu.make_async_remote_copy(
            src_ref=src, dst_ref=dst, send_sem=send, recv_sem=recv,
            device_id=device, device_id_type=MESH,
        )

    barrier = pltpu.get_barrier_semaphore()
    greeted = (
        [twin]
        + [along_a(d) for d in range(1, SIDE)]
        + [along_b(d) for d in range(1, SIDE)]
        + [along_z(d) for d in range(1, DEPTH)]
    )
    for device in greeted:
        pl.semaphore_signal(barrier, inc=1, device_id=device, device_id_type=MESH)

    images = tokens_ref.shape[0]
    starts, ends, total = [], [], jnp.int32(0)
    my_start, my_count = jnp.int32(0), jnp.int32(0)
    for i in range(images):
        starts.append(total)
        mine = owner_ref[i] == ctx
        my_start = jnp.where(mine, total, my_start)
        my_count = jnp.where(mine, tokens_ref[i], my_count)
        total = total + tokens_ref[i]
        ends.append(total)

    slots = feats_ref.shape[0]
    half = feats_ref.shape[1] // 2
    row_id = lax.broadcasted_iota(jnp.int32, (SHARE, slots), 0)
    slot_id = lax.broadcasted_iota(jnp.int32, (SHARE, slots), 1)
    distance = jnp.where(slot_id < my_count, row_id - slot_id, jnp.int32(1 << 20))

    def packed_rows(which, a_to, part_of):
        select = jnp.concatenate(
            [
                jnp.where(
                    distance == my_start - chip_of(which, a_to, b_to) * SHARE, 1.0, 0.0
                ).astype(BF16)
                for b_to in range(SIDE)
            ],
            axis=0,
        )
        columns = feats_ref[:, pl.ds(pl.multiple_of(part_of * half, half), half)]
        return jnp.dot(select, columns, preferred_element_type=F32).astype(BF16)

    for a_to in range(SIDE):
        own[a_to] = packed_rows(1 - core, a_to, 1 - core)
    pl.semaphore_wait(barrier, len(greeted))
    to_twin = [
        copy(own.at[i], sib.at[i], sib_s.at[i], sib_r.at[i], twin) for i in range(SIDE)
    ]
    for c in to_twin:
        c.start()
    for a_to in range(SIDE):
        keys_rows = packed_rows(core, a_to, core)
        first_sum[a_to] = keys_rows
    for c in to_twin:
        c.wait()
    for a_to in range(SIDE):
        first_sum[a_to] = first_sum[a_to] + sib[a_to]
    sends = [
        copy(
            first_sum.at[lax.rem(a + d, SIDE)], first_in.at[d - 1],
            first_s.at[d - 1], first_r.at[d - 1], along_a(d),
        )
        for d in range(1, SIDE)
    ]
    for c in sends:
        c.start()

    lane = lax.broadcasted_iota(jnp.int32, (SHARE, HEAD), 1)
    row = lax.broadcasted_iota(jnp.int32, (SHARE, HEAD), 0)
    begin_of, end_of = jnp.zeros_like(lane), jnp.zeros_like(lane)
    for i in range(images):
        begin_of = jnp.where(lane == i, starts[i], begin_of)
        end_of = jnp.where(lane == i, ends[i], end_of)
    for which in range(2):
        for b_to in range(SIDE):
            for a_to in range(SIDE):
                place = row + chip_of(which, a_to, b_to) * SHARE
                inside = (place >= begin_of) & (place < end_of)
                base = (b_to * SIDE + a_to) * SHARE
                hot[which, base : base + SHARE, :] = jnp.where(inside, 1.0, 0.0).astype(BF16)

    for c in sends:
        c.wait()
    block = first_sum[a]
    for d in range(1, SIDE):
        block = block + first_in[d - 1]
    for i in range(SIDE):
        own[0, i * SHARE : (i + 1) * SHARE] = block[i * SHARE : (i + 1) * SHARE]

    def share_of(i):
        return own.at[0, pl.ds(pl.multiple_of(i * SHARE, 16), SHARE)]

    sends = [
        copy(
            share_of(lax.rem(b + d, SIDE)), second_in.at[d - 1],
            second_s.at[d - 1], second_r.at[d - 1], along_b(d),
        )
        for d in range(1, SIDE)
    ]
    for c in sends:
        c.start()
    for c in sends:
        c.wait()
    block = share_of(b)[...]
    for d in range(1, SIDE):
        block = block + second_in[d - 1]
    chip_feats[core] = block
    pair = copy(chip_feats.at[core], chip_feats.at[core], pair_s.at[0], pair_r.at[0], twin)
    pair.start()
    pair.wait()

    width = weight_ref.shape[1] // 2
    blocks = width // HEAD
    columns = pl.ds(pl.multiple_of(core * width, width), width)
    product = jnp.dot(
        chip_feats[0], weight_ref[:half, columns], preferred_element_type=F32
    ) + jnp.dot(chip_feats[1], weight_ref[half:, columns], preferred_element_type=F32)
    spacing = DEPTH // blocks
    offset = core * (spacing // 2)
    for j in range(blocks):
        part[j] = product[:, j * HEAD : (j + 1) * HEAD]
    for j in range(blocks):
        home = offset + j * spacing
        d = lax.rem(home - z + DEPTH, DEPTH)

        @pl.when(d != 0)
        def _():
            copy(part.at[j], part_in.at[d], part_s.at[j], part_r.at[d], at(x, y, core, home)).start()

    is_home = lax.rem(z, spacing) == offset
    my_block = lax.div(z, spacing)

    @pl.when(is_home)
    def _():
        total = part[my_block]
        for d in range(1, DEPTH):
            copy(
                part.at[0], part_in.at[d], part_s.at[0], part_r.at[d], along_z(1)
            ).wait_recv()
        for d in range(1, DEPTH):
            total = total + part_in[d]
        scale = lax.rsqrt(jnp.mean(total * total, axis=1, keepdims=True) + EPSILON)
        normed = total * scale * gain_ref[...]
        done[...] = jnp.where(lax.rem(my_block, 2) == 0, normed, total).astype(BF16)
        for d in range(1, DEPTH):
            copy(
                done, kv.at[core, my_block, b, a], column_s.at[d - 1],
                column_r.at[my_block], along_z(d),
            ).start()
        kv[core, my_block, b, a] = done[...]

    row_copies, plane_copies, twin_copies = [], [], []
    for h in range(blocks // 2):
        pieces = pl.ds(2 * h, 2)
        row_copies.append(
            [
                copy(
                    kv.at[core, pieces, b, a], kv.at[core, pieces, b, a],
                    row_s.at[h, d - 1], row_r.at[h, d - 1], along_a(d),
                )
                for d in range(1, SIDE)
            ]
        )
        plane_copies.append(
            [
                copy(
                    kv.at[core, pieces, b], kv.at[core, pieces, b],
                    plane_s.at[h, d - 1], plane_r.at[h, d - 1], along_b(d),
                )
                for d in range(1, SIDE)
            ]
        )
        twin_copies.append(
            copy(kv.at[core, pieces], kv.at[core, pieces], twin_s.at[h], twin_r.at[h], twin)
        )

    for h in range(blocks // 2):
        for j in (2 * h, 2 * h + 1):

            @pl.when(jnp.logical_not(is_home & (my_block == j)))
            def _():
                copy(
                    done, kv.at[core, j, b, a], column_s.at[0], column_r.at[j], along_z(1)
                ).wait_recv()

        for c in row_copies[h]:
            c.start()
    for h in range(blocks // 2):
        for c in row_copies[h]:
            c.wait_recv()
        for c in plane_copies[h]:
            c.start()

    lanes = lax.broadcasted_iota(jnp.int32, mask_ref.shape[:1] + (HEAD,), 1)
    bias = jnp.zeros(lanes.shape, F32)
    for i in range(images):
        bias = jnp.where((lanes == i) & (mask_ref[:, i : i + 1] != 1), MASKED, bias)
    bias = bias.astype(BF16)
    rows = q_ref.shape[0]
    factor = HEAD**-0.5 * math.log2(math.e)

    def attend(which, h):
        keys[:, :HEAD] = kv[which, 2 * h].reshape(PACKED, HEAD)
        keys[:, HEAD:] = hot[which]

        def step(i, carry):
            head = (which * (blocks // 2) + h) * GROUP + i * STEP_HEADS
            base = pl.multiple_of(head * HEAD, HEAD)
            stacked = jnp.concatenate(
                [
                    jnp.concatenate([q_ref[:, pl.ds(base + n * HEAD, HEAD)], bias], axis=1)
                    for n in range(STEP_HEADS)
                ],
                axis=0,
            )
            scores = lax.dot_general(
                stacked, keys[...], (((1,), (1,)), ((), ())), preferred_element_type=F32
            )
            largest = jnp.maximum(jnp.max(scores, axis=1, keepdims=True), FLOOR_SCORE)
            weights = jnp.exp2(scores * factor - largest * factor)
            summed = jnp.sum(weights, axis=1, keepdims=True)
            mixed = jnp.dot(
                weights.astype(BF16), kv[which, 2 * h + 1].reshape(PACKED, HEAD),
                preferred_element_type=F32,
            )
            out = (mixed / jnp.maximum(summed, 1.0)).astype(BF16)
            for n in range(STEP_HEADS):
                o_ref[:, pl.ds(base + n * HEAD, HEAD)] = out[n * rows : (n + 1) * rows]
            return carry

        lax.fori_loop(0, GROUP // STEP_HEADS, step, 0)

    for h in range(blocks // 2):
        for c in plane_copies[h]:
            c.wait_recv()
        twin_copies[h].start()
        attend(core, h)
    for h in range(blocks // 2):
        twin_copies[h].wait_recv()
        attend(1 - core, h)

    for h in range(blocks // 2):
        twin_copies[h].wait_send()
        for c in row_copies[h] + plane_copies[h]:
            c.wait_send()
    for j in range(blocks):
        home = offset + j * spacing

        @pl.when(z != home)
        def _():
            copy(
                part.at[j], part_in.at[1], part_s.at[j], part_r.at[1], along_z(1)
            ).wait_send()

    @pl.when(is_home)
    def _():
        for d in range(1, DEPTH):
            copy(
                done, kv.at[core, my_block, b, a], column_s.at[d - 1],
                column_r.at[my_block], along_z(d),
            ).wait_send()


def shards(queries, vis_feats, kv_weight, key_gain, cross_mask, image_tokens, image_owner):
    z = lax.axis_index("head")
    rows = queries.shape[0]
    mask_rows = lax.dynamic_slice_in_dim(cross_mask, z * rows, rows, 0)
    half = vis_feats.shape[1] // 2
    blocks = kv_weight.shape[1] // (2 * HEAD)
    dma = pltpu.SemaphoreType.DMA
    whole = pl.BlockSpec(memory_space=pltpu.VMEM)
    scalars = pl.BlockSpec(memory_space=pltpu.SMEM)
    return pl.pallas_call(
        kernel,
        out_shape=jax.ShapeDtypeStruct(queries.shape, BF16),
        in_specs=[scalars, scalars, whole, whole, whole, whole, whole],
        out_specs=whole,
        scratch_shapes=[
            pltpu.VMEM((SIDE, SIDE * SHARE, half), BF16),
            pltpu.VMEM((SIDE, SIDE * SHARE, half), BF16),
            pltpu.VMEM((SIDE - 1, SIDE * SHARE, half), BF16),
            pltpu.VMEM((SIDE, SIDE * SHARE, half), BF16),
            pltpu.VMEM((SIDE - 1, SHARE, half), BF16),
            pltpu.VMEM((2, SHARE, half), BF16),
            pltpu.VMEM((blocks, SHARE, HEAD), F32),
            pltpu.VMEM((DEPTH, SHARE, HEAD), F32),
            pltpu.VMEM((SHARE, HEAD), BF16),
            pltpu.VMEM((2, blocks, SIDE, SIDE, SHARE, HEAD), BF16),
            pltpu.VMEM((2, PACKED, HEAD), BF16),
            pltpu.VMEM((PACKED, 2 * HEAD), BF16),
            dma((SIDE,)), dma((SIDE,)),
            dma((SIDE - 1,)), dma((SIDE - 1,)),
            dma((SIDE - 1,)), dma((SIDE - 1,)),
            dma((1,)), dma((1,)),
            dma((blocks,)), dma((DEPTH,)),
            dma((DEPTH - 1,)), dma((blocks,)),
            dma((blocks // 2, SIDE - 1)), dma((blocks // 2, SIDE - 1)),
            dma((blocks // 2, SIDE - 1)), dma((blocks // 2, SIDE - 1)),
            dma((blocks // 2,)), dma((blocks // 2,)),
        ],
        compiler_params=pltpu.CompilerParams(
            collective_id=0, has_side_effects=True, vmem_limit_bytes=56 * 1024 * 1024
        ),
        name="cross_attend",
    )(
        image_tokens, image_owner, vis_feats, kv_weight, key_gain.reshape(1, HEAD), mask_rows,
        queries,
    )


def solution(mesh):
    return jax.shard_map(
        shards,
        mesh=mesh,
        in_specs=(
            P(("ctx", "head"), None),
            P("ctx", "head"),
            P("head", None),
            P(),
            P("ctx", None),
            P(),
            P(),
        ),
        out_specs=P(("ctx", "head"), None),
        check_vma=False,
    )
```

time: 342 us -> 83.9 us (0.25)
  waiting for transfers between devices: 295 us -> 0 us
  Pallas kernels: 18.5 us -> 79.9 us
  between operations: 13.2 us -> 0.01 us
  other arithmetic: 6.53 us -> 0 us
  matrix products: 4.44 us -> 0 us
    psum x1 -> x0, waiting for transfers between devices: 126 us -> none  [shards(): projected = lax.psum(partial, 'head').reshape(mine.shape[0], -1, 2, HEAD)]
    reduce_scatter x1 -> x0, waiting for transfers between devices: 105 us -> none  [shards(): lax.psum_scatter(contribution, 'ctx', scatter_dimension=0, tiled=True)]
    all_gather x1 -> x0, waiting for transfers between devices: 63.9 us -> none  [shards(): lax.all_gather(kv.reshape(mine.shape[0], -1), 'ctx', axis=0, tiled=True)]
    pallas_call x1, Pallas kernels: 18.5 us -> 79.9 us  [shards(): pl.pallas_call(kernel, out_shape=jax.ShapeDtypeStruct(queries.shape, BF16...]
    dot_general x2 -> x0, matrix products: 4.44 us -> none  [the longest x1 3.38 us: shards(): jnp.dot(select.astype(jnp.bfloat16), vis_feats, preferred_element_type=jn...]
    unnamed x5 -> x4, local copies, waits for them, and re-layouts: 0.13 us -> 3.79 us
    reduce_sum x4 -> x0, other arithmetic: 3.45 us -> none  [the longest x1 1.25 us: shards(): owned = jnp.sum(jnp.where(onehot, image_owner[None, :], 0), axis=1) == ctx]
  transfers between devices with their start and end apart: 3 -> 0, of which waited for: 3 -> 0; matrix products, arithmetic and copies ran while one was open for 1% -> 0% of each run, Pallas kernels for 0% -> 0%
where the time goes in v2:
time: 83.9 us; the launch traced here: 83.7 us
  Pallas kernels  79.9 us (95%)
  local copies, waits for them, and re-layouts  3.79 us (5%)
    pallas_call x1, Pallas kernels, shards(): pl.pallas_call(kernel, out_shape=jax.ShapeDtypeStruct(queries.shape, BF16...  79.9 us
    unnamed x4, local copies, waits for them, and re-layouts  3.79 us

profile of v2, /device:TPU:1, one launch (start us, length us, event | category | flops | bytes accessed | tf_op | source)
XLA Modules:
  0.0 83.7 jit_solution(9446188828012008072)
XLA Ops:
  0.0 0.0 copy-start
  0.0 0.8 copy-done
  0.8 0.7 copy.9.mask_ref
  1.5 79.9 %cross_attend.1 = bf16[128,4096]{1,0:T(8,128)(2,1)} custom-call(s32[4]{0:T(128)} %tokens_ref.1, s32[4]{0:T(128)} %owner_ref.1, bf16[512,512]{1,0:T(8,128)(2,1)} %feats_ref.1, bf16[512,1024]{1,0:T(8,128)(2,1)} %weight_ref.1, f32[1,128]{1,0:T(1,128)} %bitcast.1, s32[128,4]{1,0:T(8,128)} %copy.9.mask_ref, bf16[128,4096]{1,0:T(8,128)(2,1)} %q_ref.1), custom_call_target="tpu_custom_call" | custom-call | tf_op jit(solution)/shard_map/cross_attend/pallas_call | solution.py:332
  81.4 2.3 %copy.11 = bf16[128,4096]{1,0:T(8,128)(2,1)} copy(bf16[128,4096]{1,0:T(8,128)(2,1)} %cross_attend.1) | data formatting | bytes 2097152
  (1 shorter events, 0.0 us)
Async XLA Ops:
  0.0 0.8 copy-start

commit v3 on v2

v3 whole, which is shorter than its diff:
```python
import math

import jax
import jax.numpy as jnp
from jax import lax
from jax.experimental import pallas as pl
from jax.experimental.pallas import tpu as pltpu
from jax.sharding import PartitionSpec as P

EPSILON = 1e-05
FLOOR_SCORE = -1e30
MASKED = -(2.0**120)
HEAD = 128
SIDE = 4
DEPTH = 16
SHARE = 80
PACKED = SHARE * SIDE * SIDE
GROUP = 8
STEP_HEADS = 4
MESH = pl.DeviceIdType.MESH
BF16, F32 = jnp.bfloat16, jnp.float32


def kernel(
    tokens_ref, owner_ref, gain_ref, mask_ref, feats_hbm, weight_hbm, q_hbm, o_ref,
    feats, weight, q_ref, own, sib, first_sum, first_in, second_out, second_in, part, part_in,
    done, kv, hot, keys, rounded, divisor,
    load_s, sib_s, sib_r, first_s, first_r, second_s, second_r,
    part_s, part_r, column_s, column_r, row_s, row_r, plane_s, plane_r, twin_s, twin_r,
):
    ctx, z = lax.axis_index("ctx"), lax.axis_index("head")
    core = lax.rem(ctx, 2)
    x = lax.rem(lax.div(ctx, 2), SIDE)
    y = lax.div(ctx, 2 * SIDE)
    a = x * (1 - core) + y * core
    b = y * (1 - core) + x * core

    def at(x_to, y_to, core_to, z_to):
        return {"ctx": (y_to * SIDE + x_to) * 2 + core_to, "head": z_to}

    def along_a(d, core_to=core):
        to = lax.rem(a + d, SIDE)
        return at(to * (1 - core) + x * core, y * (1 - core) + to * core, core_to, z)

    def along_b(d, core_to=core):
        to = lax.rem(b + d, SIDE)
        return at(x * (1 - core) + to * core, to * (1 - core) + y * core, core_to, z)

    def along_z(d):
        return at(x, y, core, lax.rem(z + d, DEPTH))

    twin = at(x, y, 1 - core, z)

    def chip_of(which, a_to, b_to):
        return (a_to * SIDE + b_to) * (1 - which) + (b_to * SIDE + a_to) * which

    def copy(src, dst, send, recv, device):
        return pltpu.make_async_remote_copy(
            src_ref=src, dst_ref=dst, send_sem=send, recv_sem=recv,
            device_id=device, device_id_type=MESH,
        )

    barrier = pltpu.get_barrier_semaphore()
    greeted = (
        [twin]
        + [along_a(d) for d in range(1, SIDE)]
        + [along_b(d) for d in range(1, SIDE)]
        + [along_a(d, 1 - core) for d in range(1, SIDE)]
        + [along_z(d) for d in range(1, DEPTH)]
    )
    for device in greeted:
        pl.semaphore_signal(barrier, inc=1, device_id=device, device_id_type=MESH)
    width = weight.shape[1]
    loads = [
        pltpu.make_async_copy(feats_hbm, feats, load_s.at[0]),
        pltpu.make_async_copy(
            weight_hbm.at[:, pl.ds(pl.multiple_of(core * width, width), width)],
            weight, load_s.at[1],
        ),
        pltpu.make_async_copy(q_hbm, q_ref, load_s.at[2]),
    ]
    for c in loads:
        c.start()

    images = tokens_ref.shape[0]
    starts, ends, total = [], [], jnp.int32(0)
    my_start, my_count = jnp.int32(0), jnp.int32(0)
    for i in range(images):
        starts.append(total)
        mine = owner_ref[i] == ctx
        my_start = jnp.where(mine, total, my_start)
        my_count = jnp.where(mine, tokens_ref[i], my_count)
        total = total + tokens_ref[i]
        ends.append(total)

    slots = feats.shape[0]
    half = feats.shape[1] // 2
    row_id = lax.broadcasted_iota(jnp.int32, (SHARE, slots), 0)
    slot_id = lax.broadcasted_iota(jnp.int32, (SHARE, slots), 1)
    distance = jnp.where(slot_id < my_count, row_id - slot_id, jnp.int32(1 << 20))

    def packed_rows(which, b_to, part_of):
        select = jnp.concatenate(
            [
                jnp.where(
                    distance == my_start - chip_of(which, a_to, b_to) * SHARE, 1.0, 0.0
                ).astype(BF16)
                for a_to in range(SIDE)
            ],
            axis=0,
        )
        columns = feats[:, pl.ds(pl.multiple_of(part_of * half, half), half)]
        rows_of = jnp.dot(select, columns, preferred_element_type=F32).astype(BF16)
        return rows_of.reshape(SIDE, SHARE, half)

    order = list(range(1, SIDE)) + [0]
    to_twin = [copy(own.at[e], sib.at[e], sib_s.at[e], sib_r.at[e], twin) for e in range(SIDE)]
    loads[0].wait()
    for n, e in enumerate(order):
        own[e] = packed_rows(1 - core, lax.rem(a + e, SIDE), 1 - core)
        if n == 0:
            pl.semaphore_wait(barrier, len(greeted))
        to_twin[e].start()
    for e in order:
        first_sum[e] = packed_rows(core, lax.rem(b + e, SIDE), core)
    first = {}
    for e in order:
        to_twin[e].wait_recv()
        first_sum[e] = first_sum[e] + sib[e]
        for d in range(1, SIDE):
            first[d, e] = copy(
                first_sum.at[e, lax.rem(a + d, SIDE)], first_in.at[d - 1, e],
                first_s.at[d - 1, e], first_r.at[d - 1, e], along_a(d),
            )
            first[d, e].start()

    lane = lax.broadcasted_iota(jnp.int32, (SHARE, HEAD), 1)
    row = lax.broadcasted_iota(jnp.int32, (SHARE, HEAD), 0)
    begin_of, end_of = jnp.zeros_like(lane), jnp.zeros_like(lane)
    for i in range(images):
        begin_of = jnp.where(lane == i, starts[i], begin_of)
        end_of = jnp.where(lane == i, ends[i], end_of)
    for which in range(2):
        for b_to in range(SIDE):
            for a_to in range(SIDE):
                place = row + chip_of(which, a_to, b_to) * SHARE
                inside = (place >= begin_of) & (place < end_of)
                base = (b_to * SIDE + a_to) * SHARE
                hot[which, base : base + SHARE, :] = jnp.where(inside, 1.0, 0.0).astype(BF16)
    bias_of = jnp.where(
        mask_ref[:, pl.ds(pl.multiple_of(z * HEAD, HEAD), HEAD)] == 1, 0.0, MASKED
    ).astype(BF16)
    same = lax.broadcasted_iota(jnp.int32, (images, HEAD), 0) == lax.broadcasted_iota(
        jnp.int32, (images, HEAD), 1
    )
    bias = lax.dot_general(
        bias_of, jnp.where(same, 1.0, 0.0).astype(BF16), (((0,), (0,)), ((), ())),
        preferred_element_type=F32,
    ).astype(BF16)

    second, arrivals = [], []
    for e in order:
        for d in range(1, SIDE):
            first[d, e].wait_recv()
        block = first_sum[e, a]
        for d in range(1, SIDE):
            block = block + first_in[d - 1, e]
        if e:
            second_out[e] = block
            source, targets = second_out.at[e], [along_b(e), along_b(e, 1 - core)]
        else:
            second_in[core, 0] = block
            source, targets = second_in.at[core, 0], [None, twin]
        for n, device in enumerate(targets):
            if device is not None:
                c = copy(
                    source, second_in.at[core, e],
                    second_s.at[n, e], second_r.at[core, e], device,
                )
                c.start()
                second.append(c)
    for which in range(2):
        for e in order:
            if e:
                copy(
                    second_out.at[e], second_in.at[which, e],
                    second_s.at[0, e], second_r.at[which, e], twin,
                ).wait_recv()
    copy(
        second_out.at[1], second_in.at[1 - core, 0], second_s.at[1, 0],
        second_r.at[1 - core, 0], twin,
    ).wait_recv()
    halves = []
    for which in range(2):
        block = second_in[which, 0]
        for e in range(1, SIDE):
            block = block + second_in[which, e]
        halves.append(block)

    blocks = width // HEAD
    spacing = DEPTH // blocks
    offset = core * (spacing // 2)
    homes = [offset + (j % 2 * 2 + j // 2) * spacing for j in range(blocks)]

    def part_sent(j):
        @pl.when(z != homes[j])
        def _():
            copy(
                part.at[j], part_in.at[1], part_s.at[j], part_r.at[1], along_z(1)
            ).wait_send()

    loads[1].wait()
    for h in range(blocks // 2):
        columns = jnp.concatenate(
            [weight[:, (2 * n + h) * HEAD : (2 * n + h + 1) * HEAD] for n in range(2)], axis=1
        )
        product = jnp.dot(halves[0], columns[:half], preferred_element_type=F32) + jnp.dot(
            halves[1], columns[half:], preferred_element_type=F32
        )
        part[2 * h] = product[:, :HEAD]
        part[2 * h + 1] = product[:, HEAD:]
        if h:
            part_sent(2 * h - 2)
            part_sent(2 * h - 1)
        for j in (2 * h, 2 * h + 1):
            home = homes[j]
            d = lax.rem(home - z + DEPTH, DEPTH)

            @pl.when(d != 0)
            def _():
                copy(
                    part.at[j], part_in.at[d], part_s.at[j], part_r.at[d], at(x, y, core, home)
                ).start()

    is_home = lax.rem(z, spacing) == offset
    place = lax.div(z, spacing)
    my_block = lax.rem(place, 2) * 2 + lax.div(place, 2)

    @pl.when(is_home)
    def _():
        total = part[my_block]
        for d in range(1, DEPTH):
            copy(
                part.at[0], part_in.at[d], part_s.at[0], part_r.at[d], along_z(1)
            ).wait_recv()
            total = total + part_in[d]
        scale = lax.rsqrt(jnp.mean(total * total, axis=1, keepdims=True) + EPSILON)
        normed = total * scale * gain_ref[...]
        done[...] = jnp.where(my_block < blocks // 2, normed, total).astype(BF16)
        for d in range(1, DEPTH):
            copy(
                done, kv.at[core, my_block, b, a], column_s.at[d - 1],
                column_r.at[my_block], along_z(d),
            ).start()
        kv[core, my_block, b, a] = done[...]

    def row_copy(h, d):
        place = kv.at[core, pl.ds(2 * h, 2), b, a]
        return copy(place, place, row_s.at[h, d - 1], row_r.at[h, d - 1], along_a(d))

    def plane_copy(h, d):
        place = kv.at[core, pl.ds(2 * h, 2), b]
        return copy(place, place, plane_s.at[h, d - 1], plane_r.at[h, d - 1], along_b(d))

    def twin_copy(h, d):
        place = kv.at[core, pl.ds(2 * h, 2), lax.rem(b - d + SIDE, SIDE)]
        return copy(place, place, twin_s.at[h, d], twin_r.at[h, d], twin)

    others = range(1, SIDE)
    for h in range(blocks // 2):
        for j in (2 * h, 2 * h + 1):

            @pl.when(jnp.logical_not(is_home & (my_block == j)))
            def _():
                copy(
                    done, kv.at[core, j, b, a], column_s.at[0], column_r.at[j], along_z(1)
                ).wait_recv()

        for d in others:
            row_copy(h, d).start()
    for h in range(blocks // 2):
        for d in others:
            row_copy(h, d).wait_recv()
        for d in others:
            plane_copy(h, d).start()
        twin_copy(h, 0).start()

    loads[2].wait()
    rows = q_ref.shape[0]
    factor = HEAD**-0.5 * math.log2(math.e)

    def forward(h):
        for d in others:
            plane_copy(h, d).wait_recv()
            twin_copy(h, d).start()

    def arrived(h):
        for d in range(SIDE):
            twin_copy(h, d).wait_recv()

    key_heads = blocks // 2
    span = STEP_HEADS * rows

    def weigh(n, carry):
        which = lax.rem(core + lax.div(n, key_heads), 2)
        h = lax.rem(n, key_heads)

        @pl.when(n == 0)
        def _():
            forward(0)

        @pl.when(n == key_heads)
        def _():
            arrived(0)

        @pl.when(n == 2 * key_heads - 1)
        def _():
            forward(1)

        keys[:, :HEAD] = kv[which, h].reshape(PACKED, HEAD)
        keys[:, HEAD:] = hot[which]
        for i in range(GROUP // STEP_HEADS):
            head = (which * key_heads + h) * GROUP + i * STEP_HEADS
            base = pl.multiple_of(head * HEAD, HEAD)
            stacked = jnp.concatenate(
                [
                    jnp.concatenate([q_ref[:, pl.ds(base + m * HEAD, HEAD)], bias], axis=1)
                    for m in range(STEP_HEADS)
                ],
                axis=0,
            )
            scores = lax.dot_general(
                stacked, keys[...], (((1,), (1,)), ((), ())), preferred_element_type=F32
            )
            largest = jnp.maximum(jnp.max(scores, axis=1, keepdims=True), FLOOR_SCORE)
            weights = jnp.exp2(scores * factor - largest * factor)
            summed = jnp.sum(weights, axis=1, keepdims=True)
            rounded[n, i * span : (i + 1) * span] = weights.astype(BF16)
            divisor[n, i * span : (i + 1) * span] = jnp.broadcast_to(
                jnp.maximum(summed, 1.0), (span, HEAD)
            )
        return carry

    def mix(n, carry):
        which = lax.rem(core + lax.div(n, key_heads), 2)
        h = lax.rem(n, key_heads)

        @pl.when(n == key_heads)
        def _():
            arrived(1)

        mixed = jnp.dot(
            rounded[n], kv[which, key_heads + h].reshape(PACKED, HEAD), preferred_element_type=F32
        )
        out = (mixed / divisor[n]).astype(BF16)
        for m in range(GROUP):
            base = pl.multiple_of(((which * key_heads + h) * GROUP + m) * HEAD, HEAD)
            o_ref[:, pl.ds(base, HEAD)] = out[m * rows : (m + 1) * rows]
        return carry

    lax.fori_loop(0, 2 * key_heads, weigh, 0)
    lax.fori_loop(0, 2 * key_heads, mix, 0)

    for h in range(blocks // 2):
        for d in others:
            row_copy(h, d).wait_send()
            if True:
                plane_copy(h, d).wait_send()
        for d in range(SIDE):
            twin_copy(h, d).wait_send()
    for j in (blocks - 2, blocks - 1):
        part_sent(j)

    @pl.when(is_home)
    def _():
        for d in range(1, DEPTH):
            copy(
                done, kv.at[core, my_block, b, a], column_s.at[d - 1],
                column_r.at[my_block], along_z(d),
            ).wait_send()

    for c in to_twin + list(first.values()) + second:
        c.wait_send()


def shards(queries, vis_feats, kv_weight, key_gain, cross_mask, image_tokens, image_owner):
    half = vis_feats.shape[1] // 2
    blocks = kv_weight.shape[1] // (2 * HEAD)
    dma = pltpu.SemaphoreType.DMA
    whole = pl.BlockSpec(memory_space=pltpu.VMEM)
    stays = pl.BlockSpec(memory_space=pltpu.HBM)
    scalars = pl.BlockSpec(memory_space=pltpu.SMEM)
    return pl.pallas_call(
        kernel,
        out_shape=pltpu.VMEM(queries.shape, BF16),
        in_specs=[scalars, scalars, whole, whole, stays, stays, stays],
        out_specs=whole,
        scratch_shapes=[
            pltpu.VMEM(vis_feats.shape, BF16),
            pltpu.VMEM((kv_weight.shape[0], kv_weight.shape[1] // 2), BF16),
            pltpu.VMEM(queries.shape, BF16),
            pltpu.VMEM((SIDE, SIDE, SHARE, half), BF16),
            pltpu.VMEM((SIDE, SIDE, SHARE, half), BF16),
            pltpu.VMEM((SIDE, SIDE, SHARE, half), BF16),
            pltpu.VMEM((SIDE - 1, SIDE, SHARE, half), BF16),
            pltpu.VMEM((SIDE, SHARE, half), BF16),
            pltpu.VMEM((2, SIDE, SHARE, half), BF16),
            pltpu.VMEM((blocks, SHARE, HEAD), F32),
            pltpu.VMEM((DEPTH, SHARE, HEAD), F32),
            pltpu.VMEM((SHARE, HEAD), BF16),
            pltpu.VMEM((2, blocks, SIDE, SIDE, SHARE, HEAD), BF16),
            pltpu.VMEM((2, PACKED, HEAD), BF16),
            pltpu.VMEM((PACKED, 2 * HEAD), BF16),
            pltpu.VMEM((blocks, GROUP * queries.shape[0], PACKED), BF16),
            pltpu.VMEM((blocks, GROUP * queries.shape[0], HEAD), F32),
            dma((3,)),
            dma((SIDE,)), dma((SIDE,)),
            dma((SIDE - 1, SIDE)), dma((SIDE - 1, SIDE)),
            dma((2, SIDE)), dma((2, SIDE)),
            dma((blocks,)), dma((DEPTH,)),
            dma((DEPTH - 1,)), dma((blocks,)),
            dma((blocks // 2, SIDE - 1)), dma((blocks // 2, SIDE - 1)),
            dma((blocks // 2, SIDE - 1)), dma((blocks // 2, SIDE - 1)),
            dma((blocks // 2, SIDE)), dma((blocks // 2, SIDE)),
        ],
        compiler_params=pltpu.CompilerParams(
            collective_id=0, has_side_effects=True, vmem_limit_bytes=56 * 1024 * 1024
        ),
        name="cross_attend",
    )(
        image_tokens, image_owner, key_gain.reshape(1, HEAD), cross_mask.T, vis_feats, kv_weight,
        queries,
    )


def solution(mesh):
    return jax.shard_map(
        shards,
        mesh=mesh,
        in_specs=(
            P(("ctx", "head"), None),
            P("ctx", "head"),
            P("head", None),
            P(),
            P("ctx", None),
            P(),
            P(),
        ),
        out_specs=P(("ctx", "head"), None),
        check_vma=False,
    )
```

time: 83.9 us -> 73.8 us (0.88)
  Pallas kernels: 79.9 us -> 72.5 us
  local copies, waits for them, and re-layouts: 3.79 us -> 0.97 us
    pallas_call x1, Pallas kernels: 79.9 us -> 72.5 us  [shards(): pl.pallas_call(kernel, out_shape=pltpu.VMEM(queries.shape, BF16), in_spec...]
    unnamed x4 -> x1, local copies, waits for them, and re-layouts: 3.79 us -> 0.97 us
where the time goes in v3:
time: 73.8 us; the launch traced here: 73.5 us
  Pallas kernels  72.5 us (98%)
  local copies, waits for them, and re-layouts  0.97 us (1%)
    pallas_call x1, Pallas kernels, shards(): pl.pallas_call(kernel, out_shape=pltpu.VMEM(queries.shape, BF16), in_spec...  72.5 us

profile of v3, /device:TPU:1, one launch (start us, length us, event | category | flops | bytes accessed | tf_op | source)
XLA Modules:
  0.0 73.5 jit_solution(9828125039518247570)
XLA Ops:
  0.0 72.5 %cross_attend.1 = bf16[128,4096]{1,0:T(8,128)(2,1)S(1)} custom-call(s32[4]{0:T(128)} %tokens_ref.1, s32[4]{0:T(128)} %owner_ref.1, f32[1,128]{1,0:T(1,128)} %bitcast.3, s32[4,2048]{1,0:T(4,128)} %bitcast.2, bf16[512,512]{1,0:T(8,128)(2,1)} %feats_hbm.1, bf16[512,1024]{1,0:T(8,128)(2,1)} %weight_hbm.1, bf16[128,4096]{1,0:T(8,128)(2,1)} %q_hbm.1), custom_call_target="tpu_custom_call" | custom-call | tf_op jit(solution)/shard_map/cross_attend/pallas_call | solution.py:393
  72.5 1.0 %copy.9 = bf16[128,4096]{1,0:T(8,128)(2,1)} copy(bf16[128,4096]{1,0:T(8,128)(2,1)S(1)} %cross_attend.1) | data formatting | bytes 2097152

commit v4 on v3

--- a/solution.py
+++ b/solution.py
@@ -68,8 +68,6 @@
         + [along_a(d, 1 - core) for d in range(1, SIDE)]
         + [along_z(d) for d in range(1, DEPTH)]
     )
-    for device in greeted:
-        pl.semaphore_signal(barrier, inc=1, device_id=device, device_id_type=MESH)
     width = weight.shape[1]
     loads = [
         pltpu.make_async_copy(feats_hbm, feats, load_s.at[0]),
@@ -79,7 +77,10 @@
         ),
         pltpu.make_async_copy(q_hbm, q_ref, load_s.at[2]),
     ]
-    for c in loads:
+    loads[0].start()
+    for device in greeted:
+        pl.semaphore_signal(barrier, inc=1, device_id=device, device_id_type=MESH)
+    for c in loads[1:]:
         c.start()
 
     images = tokens_ref.shape[0]
@@ -113,7 +114,7 @@
         rows_of = jnp.dot(select, columns, preferred_element_type=F32).astype(BF16)
         return rows_of.reshape(SIDE, SHARE, half)
 
-    order = list(range(1, SIDE)) + [0]
+    order = [2, 1, 3, 0]
     to_twin = [copy(own.at[e], sib.at[e], sib_s.at[e], sib_r.at[e], twin) for e in range(SIDE)]
     loads[0].wait()
     for n, e in enumerate(order):
@@ -127,7 +128,7 @@
     for e in order:
         to_twin[e].wait_recv()
         first_sum[e] = first_sum[e] + sib[e]
-        for d in range(1, SIDE):
+        for d in (2, 1, 3):
             first[d, e] = copy(
                 first_sum.at[e, lax.rem(a + d, SIDE)], first_in.at[d - 1, e],
                 first_s.at[d - 1, e], first_r.at[d - 1, e], along_a(d),
@@ -140,12 +141,12 @@
     for i in range(images):
         begin_of = jnp.where(lane == i, starts[i], begin_of)
         end_of = jnp.where(lane == i, ends[i], end_of)
-    for which in range(2):
+    for which, a_from in ((core, a), (1 - core, b)):
         for b_to in range(SIDE):
-            for a_to in range(SIDE):
-                place = row + chip_of(which, a_to, b_to) * SHARE
+            for e in range(SIDE):
+                place = row + chip_of(which, lax.rem(a_from + e, SIDE), b_to) * SHARE
                 inside = (place >= begin_of) & (place < end_of)
-                base = (b_to * SIDE + a_to) * SHARE
+                base = (b_to * SIDE + e) * SHARE
                 hot[which, base : base + SHARE, :] = jnp.where(inside, 1.0, 0.0).astype(BF16)
     bias_of = jnp.where(
         mask_ref[:, pl.ds(pl.multiple_of(z * HEAD, HEAD), HEAD)] == 1, 0.0, MASKED
@@ -247,42 +248,49 @@
         scale = lax.rsqrt(jnp.mean(total * total, axis=1, keepdims=True) + EPSILON)
         normed = total * scale * gain_ref[...]
         done[...] = jnp.where(my_block < blocks // 2, normed, total).astype(BF16)
-        for d in range(1, DEPTH):
+        for d in sorted(range(1, DEPTH), key=lambda d: -min(d, DEPTH - d)):
             copy(
-                done, kv.at[core, my_block, b, a], column_s.at[d - 1],
+                done, kv.at[core, my_block, b, 0], column_s.at[d - 1],
                 column_r.at[my_block], along_z(d),
             ).start()
-        kv[core, my_block, b, a] = done[...]
+        kv[core, my_block, b, 0] = done[...]
 
     def row_copy(h, d):
-        place = kv.at[core, pl.ds(2 * h, 2), b, a]
-        return copy(place, place, row_s.at[h, d - 1], row_r.at[h, d - 1], along_a(d))
-
-    def plane_copy(h, d):
-        place = kv.at[core, pl.ds(2 * h, 2), b]
-        return copy(place, place, plane_s.at[h, d - 1], plane_r.at[h, d - 1], along_b(d))
+        pieces = pl.ds(2 * h, 2)
+        return copy(
+            kv.at[core, pieces, b, 0], kv.at[core, pieces, b, SIDE - d],
+            row_s.at[h, d - 1], row_r.at[h, d - 1], along_a(d),
+        )
+
+    def plane_copy(h, d, later):
+        place = kv.at[core, pl.ds(2 * h, 2), b, pl.ds(1, SIDE - 1) if later else pl.ds(0, 1)]
+        return copy(
+            place, place, plane_s.at[h, later, d - 1], plane_r.at[h, later, d - 1], along_b(d)
+        )
 
     def twin_copy(h, d):
         place = kv.at[core, pl.ds(2 * h, 2), lax.rem(b - d + SIDE, SIDE)]
         return copy(place, place, twin_s.at[h, d], twin_r.at[h, d], twin)
 
-    others = range(1, SIDE)
+    others = sorted(range(1, SIDE), key=lambda d: -min(d, SIDE - d))
     for h in range(blocks // 2):
         for j in (2 * h, 2 * h + 1):
 
             @pl.when(jnp.logical_not(is_home & (my_block == j)))
             def _():
                 copy(
-                    done, kv.at[core, j, b, a], column_s.at[0], column_r.at[j], along_z(1)
+                    done, kv.at[core, j, b, 0], column_s.at[0], column_r.at[j], along_z(1)
                 ).wait_recv()
 
         for d in others:
             row_copy(h, d).start()
+        for d in others:
+            plane_copy(h, d, 0).start()
     for h in range(blocks // 2):
         for d in others:
             row_copy(h, d).wait_recv()
         for d in others:
-            plane_copy(h, d).start()
+            plane_copy(h, d, 1).start()
         twin_copy(h, 0).start()
 
     loads[2].wait()
@@ -291,7 +299,8 @@
 
     def forward(h):
         for d in others:
-            plane_copy(h, d).wait_recv()
+            plane_copy(h, d, 0).wait_recv()
+            plane_copy(h, d, 1).wait_recv()
             twin_copy(h, d).start()
 
     def arrived(h):
@@ -313,7 +322,7 @@
         def _():
             arrived(0)
 
-        @pl.when(n == 2 * key_heads - 1)
+        @pl.when(n == key_heads)
         def _():
             forward(1)
 
@@ -364,8 +373,8 @@
     for h in range(blocks // 2):
         for d in others:
             row_copy(h, d).wait_send()
-            if True:
-                plane_copy(h, d).wait_send()
+            for later in range(2):
+                plane_copy(h, d, later).wait_send()
         for d in range(SIDE):
             twin_copy(h, d).wait_send()
     for j in (blocks - 2, blocks - 1):
@@ -375,7 +384,7 @@
     def _():
         for d in range(1, DEPTH):
             copy(
-                done, kv.at[core, my_block, b, a], column_s.at[d - 1],
+                done, kv.at[core, my_block, b, 0], column_s.at[d - 1],
                 column_r.at[my_block], along_z(d),
             ).wait_send()
 
@@ -420,7 +429,7 @@
             dma((blocks,)), dma((DEPTH,)),
             dma((DEPTH - 1,)), dma((blocks,)),
             dma((blocks // 2, SIDE - 1)), dma((blocks // 2, SIDE - 1)),
-            dma((blocks // 2, SIDE - 1)), dma((blocks // 2, SIDE - 1)),
+            dma((blocks // 2, 2, SIDE - 1)), dma((blocks // 2, 2, SIDE - 1)),
             dma((blocks // 2, SIDE)), dma((blocks // 2, SIDE)),
         ],
         compiler_params=pltpu.CompilerParams(

time: 73.8 us -> 69.6 us (0.943)
  Pallas kernels: 72.5 us -> 68.1 us
    pallas_call x1, Pallas kernels: 72.5 us -> 68.1 us  [shards(): pl.pallas_call(kernel, out_shape=pltpu.VMEM(queries.shape, BF16), in_spec...]
where the time goes in v4:
time: 69.6 us; the launch traced here: 69.1 us
  Pallas kernels  68.1 us (98%)
  local copies, waits for them, and re-layouts  0.97 us (1%)
    pallas_call x1, Pallas kernels, shards(): pl.pallas_call(kernel, out_shape=pltpu.VMEM(queries.shape, BF16), in_spec...  68.1 us

profile of v4, /device:TPU:1, one launch (start us, length us, event | category | flops | bytes accessed | tf_op | source)
XLA Modules:
  0.0 69.1 jit_solution(5578273947290321801)
XLA Ops:
  0.0 68.1 %cross_attend.1 = bf16[128,4096]{1,0:T(8,128)(2,1)S(1)} custom-call(s32[4]{0:T(128)} %tokens_ref.1, s32[4]{0:T(128)} %owner_ref.1, f32[1,128]{1,0:T(1,128)} %bitcast.3, s32[4,2048]{1,0:T(4,128)} %bitcast.2, bf16[512,512]{1,0:T(8,128)(2,1)} %feats_hbm.1, bf16[512,1024]{1,0:T(8,128)(2,1)} %weight_hbm.1, bf16[128,4096]{1,0:T(8,128)(2,1)} %q_hbm.1), custom_call_target="tpu_custom_call" | custom-call | tf_op jit(solution)/shard_map/cross_attend/pallas_call | solution.py:402
  68.1 1.0 %copy.9 = bf16[128,4096]{1,0:T(8,128)(2,1)} copy(bf16[128,4096]{1,0:T(8,128)(2,1)S(1)} %cross_attend.1) | data formatting | bytes 2097152

commit v5 on v4

--- a/solution.py
+++ b/solution.py
@@ -122,12 +122,11 @@
         if n == 0:
             pl.semaphore_wait(barrier, len(greeted))
         to_twin[e].start()
-    for e in order:
-        first_sum[e] = packed_rows(core, lax.rem(b + e, SIDE), core)
     first = {}
     for e in order:
+        packed = packed_rows(core, lax.rem(b + e, SIDE), core)
         to_twin[e].wait_recv()
-        first_sum[e] = first_sum[e] + sib[e]
+        first_sum[e] = packed + sib[e]
         for d in (2, 1, 3):
             first[d, e] = copy(
                 first_sum.at[e, lax.rem(a + d, SIDE)], first_in.at[d - 1, e],

time: 69.6 us -> 69 us (level)
  no operation moved by 1% of the time
where the time goes in v5:
time: 69 us; the launch traced here: 68.7 us
  Pallas kernels  67.7 us (98%)
  local copies, waits for them, and re-layouts  0.97 us (1%)
    pallas_call x1, Pallas kernels, shards(): pl.pallas_call(kernel, out_shape=pltpu.VMEM(queries.shape, BF16), in_spec...  67.7 us

profile of v5, /device:TPU:1, one launch (start us, length us, event | category | flops | bytes accessed | tf_op | source)
XLA Modules:
  0.0 68.7 jit_solution(9115067874958901623)
XLA Ops:
  0.0 67.7 %cross_attend.1 = bf16[128,4096]{1,0:T(8,128)(2,1)S(1)} custom-call(s32[4]{0:T(128)} %tokens_ref.1, s32[4]{0:T(128)} %owner_ref.1, f32[1,128]{1,0:T(1,128)} %bitcast.3, s32[4,2048]{1,0:T(4,128)} %bitcast.2, bf16[512,512]{1,0:T(8,128)(2,1)} %feats_hbm.1, bf16[512,1024]{1,0:T(8,128)(2,1)} %weight_hbm.1, bf16[128,4096]{1,0:T(8,128)(2,1)} %q_hbm.1), custom_call_target="tpu_custom_call" | custom-call | tf_op jit(solution)/shard_map/cross_attend/pallas_call | solution.py:401
  67.7 1.0 %copy.9 = bf16[128,4096]{1,0:T(8,128)(2,1)} copy(bf16[128,4096]{1,0:T(8,128)(2,1)S(1)} %cross_attend.1) | data formatting | bytes 2097152

commit v6 on v5

--- a/solution.py
+++ b/solution.py
@@ -61,13 +61,11 @@
         )
 
     barrier = pltpu.get_barrier_semaphore()
-    greeted = (
-        [twin]
-        + [along_a(d) for d in range(1, SIDE)]
-        + [along_b(d) for d in range(1, SIDE)]
-        + [along_a(d, 1 - core) for d in range(1, SIDE)]
-        + [along_z(d) for d in range(1, DEPTH)]
-    )
+    far_first = sorted(range(1, DEPTH), key=lambda d: -min(d, DEPTH - d))
+    greeted = [along_z(d) for d in far_first]
+    for d in (2, 1, 3):
+        greeted += [along_a(d), along_b(d), along_a(d, 1 - core)]
+    greeted.append(twin)
     width = weight.shape[1]
     loads = [
         pltpu.make_async_copy(feats_hbm, feats, load_s.at[0]),

time: 69 us -> 69.4 us (level); the launches traced: 68.7 us -> 68.3 us
  no operation moved by 1% of the time
where the time goes in v6:
time: 69.4 us; the launch traced here: 68.3 us
  Pallas kernels  67.3 us (97%)
  local copies, waits for them, and re-layouts  0.97 us (1%)
    pallas_call x1, Pallas kernels, shards(): pl.pallas_call(kernel, out_shape=pltpu.VMEM(queries.shape, BF16), in_spec...  67.3 us

profile of v6, /device:TPU:1, one launch (start us, length us, event | category | flops | bytes accessed | tf_op | source)
XLA Modules:
  0.0 68.3 jit_solution(17540766052432844164)
XLA Ops:
  0.0 67.3 %cross_attend.1 = bf16[128,4096]{1,0:T(8,128)(2,1)S(1)} custom-call(s32[4]{0:T(128)} %tokens_ref.1, s32[4]{0:T(128)} %owner_ref.1, f32[1,128]{1,0:T(1,128)} %bitcast.3, s32[4,2048]{1,0:T(4,128)} %bitcast.2, bf16[512,512]{1,0:T(8,128)(2,1)} %feats_hbm.1, bf16[512,1024]{1,0:T(8,128)(2,1)} %weight_hbm.1, bf16[128,4096]{1,0:T(8,128)(2,1)} %q_hbm.1), custom_call_target="tpu_custom_call" | custom-call | tf_op jit(solution)/shard_map/cross_attend/pallas_call | solution.py:399
  67.4 1.0 %copy.9 = bf16[128,4096]{1,0:T(8,128)(2,1)} copy(bf16[128,4096]{1,0:T(8,128)(2,1)S(1)} %cross_attend.1) | data formatting | bytes 2097152
